TPU v7x, 32 devices: a whole 2x2x4 slice. The times are simulated.
32 devices in a mesh: groups: 2 (over y), col: 4 (over z), row: 4 (over x, core).
Axes of the slice: x: 2, y: 2, z: 4, core: 2. Of those that a mesh axis runs over, the one named last changes fastest.
Arguments:
- x_stored: bfloat16 [1024, 9216], P(('groups', 'row'), 'col'), parts along dimension 0, may hold values from -6 to 6
- group_units: int32 [64], replicated, may hold values from 1 to 12, 288 in all
- group_order: int32 [64], replicated, may hold values from 0 to 63, each once
- up_weight: bfloat16 [9216, 36864], P('row', 'col'), may hold values from -0.0625 to 0.0625
- down_weight: bfloat16 [36864, 9216], P('col', 'row'), may hold values from -0.03125 to 0.03125
Outputs:
- mixed: bfloat16 [1024, 9216], P(('groups', 'col'), 'row'), parts along dimension 0
There are 2 independent parts, one for each index of `groups`. A program takes and returns all parts, laid end to end along the dimension named above; an argument that names none is the same for every part. Nothing has to cross between parts.
Inputs may be any that keep to these rules, and one draw needn't show every extreme that they name: `group_units`: sizes in blocks of 32 features; they sum to 288, and one group has exactly 12. `group_order`: each group number appears once.
All inputs are finite; a program needn't handle non-finite values.
Results may differ from a plain program's by a relative error of at most 0.0095.
Values may be sent and summed in bfloat16 or wider, within the bound.
A program may use at most 256 MiB of HBM per device.

v0:
```python
import jax
import jax.numpy as jnp
from jax import lax
from jax.sharding import PartitionSpec as P

BLOCK = 32
UNITS = 288


def unit_source(group_units, group_order):
    count = group_units.shape[0]
    group_ids = jnp.arange(count, dtype=jnp.int32)
    onehot = (group_order[:, None] == group_ids[None, :]).astype(jnp.int32)
    canon_start = jnp.cumsum(group_units) - group_units
    slot_length = jnp.sum(onehot * group_units[None, :], axis=1)
    slot_canon = jnp.sum(onehot * canon_start[None, :], axis=1)
    slot_start = jnp.cumsum(slot_length) - slot_length
    unit_ids = jnp.arange(UNITS, dtype=jnp.int32)
    inside = (unit_ids[:, None] >= slot_start[None, :]) & (
        unit_ids[:, None] < (slot_start + slot_length)[None, :]
    )
    canon_unit = jnp.sum(
        jnp.where(inside, slot_canon[None, :] + unit_ids[:, None] - slot_start[None, :], 0), axis=1
    )
    source = jnp.sum(
        jnp.where(canon_unit[None, :] == unit_ids[:, None], unit_ids[None, :], 0), axis=1
    )
    return source


def column_list(source):
    offsets = jnp.arange(BLOCK, dtype=jnp.int32)
    return (source[:, None] * BLOCK + offsets[None, :]).reshape(-1)


def exponent_floor(magnitude, lowest, highest, offset):
    result = jnp.full(magnitude.shape, 2.0 ** (lowest + offset), jnp.float32)
    for power in range(lowest + 1, highest + 1):
        result = jnp.where(magnitude >= 2.0**power, jnp.float32(2.0 ** (power + offset)), result)
    return result


def encode(values):
    row_total = values.shape[0]
    blocks = values.astype(jnp.float32).reshape(row_total, -1, BLOCK)
    largest = jnp.max(jnp.abs(blocks), axis=2)
    scale = exponent_floor(largest, -20, 8, -8)
    magnitude = jnp.abs(blocks) / scale[:, :, None]
    spacing = exponent_floor(magnitude, -6, 8, -3)
    level = jnp.minimum(jnp.floor(magnitude / spacing + 0.5) * spacing, 448.0)
    encoded = jnp.where(blocks < 0.0, -level, level).astype(jnp.bfloat16)
    return (encoded.reshape(row_total, -1), scale.astype(jnp.bfloat16))


def decode(encoded, scales):
    row_total = encoded.shape[0]
    blocks = (
        encoded.astype(jnp.float32).reshape(row_total, -1, BLOCK)
        * scales.astype(jnp.float32)[:, :, None]
    )
    return blocks.astype(jnp.bfloat16).reshape(row_total, -1)


def squared(values):
    return jnp.square(jnp.maximum(values, 0.0)).astype(jnp.bfloat16)


def on_device(x_stored, group_units, group_order, up_weight, down_weight):
    source = unit_source(group_units, group_order)
    stored = lax.all_gather(x_stored, "col", axis=1, tiled=True)
    encoded, scales = encode(jnp.take(stored, column_list(source), axis=1))
    encoded, scales = (
        lax.all_to_all(encoded, "row", split_axis=1, concat_axis=0, tiled=True),
        lax.all_to_all(scales, "row", split_axis=1, concat_axis=0, tiled=True),
    )
    panels = decode(encoded, scales)
    shares = lax.psum_scatter(
        jnp.dot(panels, up_weight, preferred_element_type=jnp.float32),
        "row",
        scatter_dimension=0,
        tiled=True,
    )
    hidden = lax.all_gather(squared(shares), "row", axis=0, tiled=True)
    mixed = lax.psum_scatter(
        jnp.dot(hidden, down_weight, preferred_element_type=jnp.float32).astype(jnp.bfloat16),
        "col",
        scatter_dimension=0,
        tiled=True,
    )
    return mixed


def solution(mesh):
    in_specs = (P(("groups", "row"), "col"), P(), P(), P("row", "col"), P("col", "row"))
    out_specs = P(("groups", "col"), "row")
    return jax.shard_map(
        on_device, mesh=mesh, in_specs=in_specs, out_specs=out_specs, check_vma=False
    )
```

profile of v0, /device:TPU:25, one launch (start us, length us, event | category | flops | bytes accessed | tf_op | source)
XLA Modules:
  0.0 466.4 jit_solution(246350163177016266)
XLA Ops:
  6.5 2.1 copy.22
  8.7 0.7 copy.21
  9.6 0.7 sub.17
  10.3 0.8 select_reduce_fusion.3
  12.7 45.5 %all-gather.3.cloned.1.call-done = bf16[128,9216]{0,1:T(8,128)(2,1)} async-done(((bf16[128,2304]{0,1:T(8,128)(2,1)}), bf16[128,9216]{0,1:T(8,128)(2,1)}) %all-gather.3.cloned.1.call-update) | async-done | bytes 2359312 | tf_op jit(solution)/shard_map/all_gather | solution.py:70
  58.2 26.5 %gather_fusion = bf16[9216,128]{1,0:T(8,128)(2,1)S(1)} fusion(bf16[128,9216]{0,1:T(8,128)(2,1)} %all-gather.3.cloned.1.call-done, s32[9216]{0:T(1024)S(1)} %broadcast_clamp_fusion), kind=kCustom, calls=%fused_computation | custom fusion | bytes 4755456 | tf_op jit(solution)/shard_map/jit(_take)/gather | solution.py:71
  84.7 1.8 abs_reduce_fusion
  86.7 0.5 select_select_fusion
  87.3 0.8 select_convert_fusion
  88.1 3.7 all-to-all-start.1
  92.1 8.7 %fusion.6 = bf16[128,4,2304]{0,2,1:T(8,128)(2,1)} fusion(bf16[128,4,2304]{0,2,1:T(8,128)(2,1)S(1)} %bitcast.50, pred[4,2304]{1,0:T(4,128)(4,1)S(1)} %compare_and_fusion.1, f32[128,4,2304]{0,2,1:T(8,128)S(1)} %bitcast.51), kind=kLoop, calls=%fused_computation.16 | loop fusion | flops 49545216 | bytes 9446400 | tf_op jit(solution)/shard_map/convert_element_type | solution.py:51
  100.9 3.6 all-to-all-start
  104.6 2.8 mul.55
  107.3 6.1 %copy.25 = f32[512,2304]{1,0:T(8,128)} copy(f32[512,2304]{0,1:T(8,128)} %bitcast.52) | data formatting | bytes 9437184 | tf_op jit(solution)/shard_map/mul | solution.py:58
  113.4 18.7 %all-to-all-done = bf16[128,4,2304]{0,2,1:T(8,128)(2,1)S(1)} async-done(((bf16[128,4,2304]{0,2,1:T(8,128)(2,1)}), bf16[128,4,2304]{0,2,1:T(8,128)(2,1)S(1)}, u32[]{:S(2)}, u32[]{:S(2)}) %all-to-all-start) | async-done | bytes 2359328 | tf_op jit(solution)/shard_map/all_to_all | solution.py:73
  132.2 2.5 convert_bitcast_fusion
  134.7 6.1 %copy.23 = f32[4,128,2304]{2,1,0:T(8,128)} copy(f32[4,128,2304]{1,2,0:T(8,128)} %convert_bitcast_fusion) | data formatting | bytes 9437184 | tf_op jit(solution)/shard_map/convert_element_type | solution.py:58
  140.8 4.2 fusion.5
  145.0 30.4 %fusion.8 = f32[512,9216]{1,0:T(8,128)} fusion(bf16[512,2304]{1,0:T(8,128)(2,1)S(1)} %fusion.5, bf16[2304,9216]{1,0:T(8,128)(2,1)} %param.8), kind=kOutput, calls=%fused_computation.53 | convolution fusion | flops 21743271936 | bytes 63700992 | tf_op jit(solution)/shard_map/dot_general | solution.py:78
  175.5 140.1 %reduce-scatter.3.cloned.1.call-done = f32[128,9216]{1,0:T(8,128)} async-done(((f32[512,9216]{1,0:T(8,128)}), f32[128,9216]{1,0:T(8,128)}) %reduce-scatter.3.cloned.1.call-update) | async-done | bytes 4718608 | tf_op jit(solution)/shard_map/reduce_scatter | solution.py:77
  315.6 4.2 multiply_convert_fusion
  320.0 64.6 %all-gather.5.cloned.1.call-done = bf16[512,9216]{1,0:T(8,128)(2,1)} async-done(((bf16[128,9216]{1,0:T(8,128)(2,1)}), bf16[512,9216]{1,0:T(8,128)(2,1)}) %all-gather.5.cloned.1.call-update) | async-done | bytes 9437200 | tf_op jit(solution)/shard_map/all_gather | solution.py:83
  384.6 29.0 %convolution_convert_fusion = bf16[512,2304]{1,0:T(8,128)(2,1)} fusion(bf16[512,9216]{1,0:T(8,128)(2,1)} %all-gather.5.cloned.1.call-done, bf16[9216,2304]{1,0:T(8,128)(2,1)} %param.9), kind=kOutput, calls=%fused_computation.17 | convolution fusion | flops 21744451584 | bytes 54263808 | tf_op jit(solution)/shard_map/dot_general | solution.py:85
  413.6 46.2 %reduce-scatter.5.cloned.1.call-done = bf16[128,2304]{1,0:T(8,128)(2,1)} async-done(((bf16[512,2304]{1,0:T(8,128)(2,1)}), bf16[128,2304]{1,0:T(8,128)(2,1)}) %reduce-scatter.5.cloned.1.call-update) | async-done | bytes 589840 | tf_op jit(solution)/shard_map/reduce_scatter | solution.py:84
  (32 shorter events, 2.5 us)
Async XLA Ops:
  6.5 51.7 %all-gather.3.cloned.1.call-start = ((), (), s32[]{:S(2)}) async-start(), calls=%async_computation.4 | async-start | bytes 2949120 | tf_op jit(solution)/shard_map/all_gather | solution.py:70
  88.1 12.8 %all-to-all-start.1 = ((bf16[128,4,72]{0,2,1:T(8,128)(2,1)}), bf16[128,4,72]{0,2,1:T(8,128)(2,1)S(1)}, u32[]{:S(2)}, u32[]{:S(2)}) async-start(bf16[128,4,72]{0,2,1:T(8,128)(2,1)} %select_convert_fusion), calls=%async_computation.1 | async-start | bytes 147456 | tf_op jit(solution)/shard_map/all_to_all | solution.py:74
  100.9 31.3 %all-to-all-start = ((bf16[128,4,2304]{0,2,1:T(8,128)(2,1)}), bf16[128,4,2304]{0,2,1:T(8,128)(2,1)S(1)}, u32[]{:S(2)}, u32[]{:S(2)}) async-start(bf16[128,4,2304]{0,2,1:T(8,128)(2,1)} %fusion.6), calls=%async_computation | async-start | bytes 4718592 | tf_op jit(solution)/shard_map/all_to_all | solution.py:73
  104.5 211.1 %reduce-scatter.3.cloned.1.call-start = ((), (), s32[]{:S(2)}) async-start(), calls=%async_computation.5 | async-start | bytes 23592960 | tf_op jit(solution)/shard_map/reduce_scatter | solution.py:77
  175.4 209.2 %all-gather.5.cloned.1.call-start = ((), (), s32[]{:S(2)}) async-start(), calls=%async_computation.6 | async-start | bytes 11796480 | tf_op jit(solution)/shard_map/all_gather | solution.py:83
  319.8 140.0 %reduce-scatter.5.cloned.1.call-start = ((), (), s32[]{:S(2)}) async-start(), calls=%async_computation.7 | async-start | bytes 2949120 | tf_op jit(solution)/shard_map/reduce_scatter | solution.py:84
Sparse Core Ops, SparseCore 0:
  8.9 49.2 all-gather.2
  175.5 140.0 reduce-scatter.2
  319.9 64.6 all-gather.4
  413.7 46.0 reduce-scatter.4
where the time goes:
time: 470 us; the launch traced here: 466 us
  waiting for transfers between devices  315 us (67%)
  matrix products  59.3 us (13%)
  local copies, waits for them, and re-layouts  45.3 us (10%)
  other arithmetic  25.5 us (5%)
  between operations  13.3 us (3%)
  starting transfers between devices  7.65 us (2%)
    reduce_scatter x1, waiting for transfers between devices, on_device(): lax.psum_scatter(jnp.dot(panels, up_weight, preferred_element_type=jnp.fl...  140 us
    all_gather x1, waiting for transfers between devices, on_device(): hidden = lax.all_gather(squared(shares), 'row', axis=0, tiled=True)  64.6 us
    reduce_scatter x1, waiting for transfers between devices, on_device(): lax.psum_scatter(jnp.dot(hidden, down_weight, preferred_element_type=jnp....  46.2 us
    all_gather x1, waiting for transfers between devices, on_device(): stored = lax.all_gather(x_stored, 'col', axis=1, tiled=True)  45.5 us
    dot_general x1, matrix products, on_device(): jnp.dot(panels, up_weight, preferred_element_type=jnp.float32)  30.4 us
    dot_general x1, matrix products, on_device(): jnp.dot(hidden, down_weight, preferred_element_type=jnp.float32)  29 us
    gather x1, local copies, waits for them, and re-layouts, on_device(): encoded, scales = encode(jnp.take(stored, column_list(source), axis=1))  26.5 us
    all_to_all x1, waiting for transfers between devices, on_device(): lax.all_to_all(encoded, 'row', split_axis=1, concat_axis=0, tiled=True)  18.7 us
  transfers between devices with their start and end apart: 6, of which 5 were waited for; matrix products, arithmetic and copies ran while one was open for 5% of the time, Pallas kernels for 0%

commit v1 on v0

v1 whole, which is shorter than its diff:
```python
import functools
import jax
import jax.numpy as jnp
from jax import lax
from jax.experimental import pallas as pl
from jax.experimental.pallas import tpu as pltpu
from jax.sharding import PartitionSpec as P

BLOCK = 32
UNITS = 288
MESH = pl.DeviceIdType.MESH
LAG = 5


def unit_source(group_units, group_order):
    count = group_units.shape[0]
    group_ids = jnp.arange(count, dtype=jnp.int32)
    onehot = (group_order[:, None] == group_ids[None, :]).astype(jnp.int32)
    canon_start = jnp.cumsum(group_units) - group_units
    slot_length = jnp.sum(onehot * group_units[None, :], axis=1)
    slot_canon = jnp.sum(onehot * canon_start[None, :], axis=1)
    slot_start = jnp.cumsum(slot_length) - slot_length
    unit_ids = jnp.arange(UNITS, dtype=jnp.int32)
    inside = (unit_ids[:, None] >= slot_start[None, :]) & (
        unit_ids[:, None] < (slot_start + slot_length)[None, :]
    )
    canon_unit = jnp.sum(
        jnp.where(inside, slot_canon[None, :] + unit_ids[:, None] - slot_start[None, :], 0), axis=1
    )
    source = jnp.sum(
        jnp.where(canon_unit[None, :] == unit_ids[:, None], unit_ids[None, :], 0), axis=1
    )
    return source


def exponent_floor(magnitude, lowest, highest, offset):
    result = jnp.full(magnitude.shape, 2.0 ** (lowest + offset), jnp.float32)
    for power in range(lowest + 1, highest + 1):
        result = jnp.where(magnitude >= 2.0**power, jnp.float32(2.0 ** (power + offset)), result)
    return result


def block_scaled(values):
    features, tokens = values.shape
    blocks = values.astype(jnp.float32).reshape(features // BLOCK, BLOCK, tokens)
    largest = jnp.max(jnp.abs(blocks), axis=1)
    scale = exponent_floor(largest, -20, 8, -8)[:, None, :]
    magnitude = jnp.abs(blocks) / scale
    spacing = exponent_floor(magnitude, -6, 8, -3)
    level = jnp.minimum(jnp.floor(magnitude / spacing + 0.5) * spacing, 448.0)
    panels = jnp.where(blocks < 0.0, -level, level) * scale
    return panels.astype(jnp.bfloat16)


def middle_kernel(passes, chunks, width, panel_ref, up_ref, down_ref, out_ref,
                  near, hand, far, hid, total, up_buf, down_buf,
                  up_sem, down_sem, near_send, near_recv, far_send, far_recv, hid_send, hid_recv):
    items = passes * chunks
    half = near.shape[1]
    row = lax.axis_index("row")
    sibling = row + 1 - 2 * lax.rem(row, 2)
    partner = lax.rem(row + 2, 4)

    barrier = pltpu.get_barrier_semaphore()
    for other in (sibling, partner):
        pl.semaphore_signal(barrier, inc=1, device_id={"row": other}, device_id_type=MESH)

    def up_copy(item):
        slot = lax.rem(item, 2)
        columns = pl.ds(pl.multiple_of(lax.rem(item, chunks) * width, width), width)
        return pltpu.make_async_copy(up_ref.at[:, columns], up_buf.at[slot], up_sem.at[slot])

    def down_copy(item):
        slot = lax.rem(item, 2)
        rows = pl.ds(pl.multiple_of(lax.rem(item, chunks) * width, width), width)
        return pltpu.make_async_copy(down_ref.at[rows, :], down_buf.at[slot], down_sem.at[slot])

    def to_near(item):
        return pltpu.make_async_remote_copy(
            src_ref=near.at[item], dst_ref=hand.at[item], send_sem=near_send.at[item],
            recv_sem=near_recv.at[item], device_id={"row": sibling}, device_id_type=MESH)

    def to_far(item):
        return pltpu.make_async_remote_copy(
            src_ref=far.at[item], dst_ref=hid.at[item, 0], send_sem=far_send.at[item],
            recv_sem=far_recv.at[item], device_id={"row": partner}, device_id_type=MESH)

    def to_hid(item):
        return pltpu.make_async_remote_copy(
            src_ref=hid.at[item, 0], dst_ref=hid.at[item, 1], send_sem=hid_send.at[item],
            recv_sem=hid_recv.at[item], device_id={"row": sibling}, device_id_type=MESH)

    up_copy(0).start()
    up_copy(1).start()
    down_copy(0).start()
    down_copy(1).start()
    pl.semaphore_wait(barrier, 2)

    def step(t, carry):
        @pl.when(t < items)
        def _():
            up_copy(t).wait()
            slot = lax.rem(t, 2)
            product = jnp.dot(panel_ref[lax.div(t, chunks)], up_buf[slot],
                              preferred_element_type=jnp.float32)
            near[t] = product[half:].astype(jnp.bfloat16)
            to_near(t).start()
            far[t] = product[:half].astype(jnp.bfloat16)

            @pl.when(t + 2 < items)
            def _():
                up_copy(t + 2).start()

        @pl.when((t >= 1) & (t < items + 1))
        def _():
            item = t - 1
            to_near(item).wait_recv()
            far[item] = (far[item].astype(jnp.float32) + hand[item].astype(jnp.float32)).astype(jnp.bfloat16)
            to_far(item).start()

        @pl.when((t >= LAG) & (t < items + LAG))
        def _():
            item = t - LAG
            to_far(item).wait_recv()
            summed = far[item].astype(jnp.float32) + hid[item, 0].astype(jnp.float32)
            hid[item, 0] = jnp.square(jnp.maximum(summed, 0.0)).astype(jnp.bfloat16)
            to_hid(item).start()

        @pl.when(t >= LAG + 1)
        def _():
            item = t - LAG - 1
            slot = lax.rem(item, 2)
            place = lax.rem(item, chunks)
            to_hid(item).wait_recv()
            down_copy(item).wait()
            product = jnp.dot(hid[item].reshape(2 * half, width), down_buf[slot],
                              preferred_element_type=jnp.float32)

            @pl.when(place == 0)
            def _():
                total[...] = product

            @pl.when(place > 0)
            def _():
                total[...] += product

            @pl.when(item + 2 < items)
            def _():
                down_copy(item + 2).start()

            @pl.when(place == chunks - 1)
            def _():
                out_ref[lax.div(item, chunks)] = total[...].astype(jnp.bfloat16)

        return carry

    lax.fori_loop(0, items + LAG + 1, step, 0)

    def drain(item, carry):
        to_near(item).wait_send()
        to_far(item).wait_send()
        to_hid(item).wait_send()
        return carry

    lax.fori_loop(0, items, drain, 0)


def middle(panels, up_weight, down_weight):
    passes, tokens, depth = panels.shape
    hidden = up_weight.shape[1]
    columns = down_weight.shape[1]
    width = next(w for w in (512, 384, 256, 128) if hidden % w == 0)
    chunks = hidden // width
    items = passes * chunks
    half = tokens // 2
    flops = 2 * passes * tokens * hidden * (depth + columns)
    return pl.pallas_call(
        functools.partial(middle_kernel, passes, chunks, width),
        out_shape=jax.ShapeDtypeStruct((passes, tokens, columns), jnp.bfloat16),
        in_specs=[pl.BlockSpec(memory_space=pltpu.VMEM), pl.BlockSpec(memory_space=pl.ANY),
                  pl.BlockSpec(memory_space=pl.ANY)],
        out_specs=pl.BlockSpec(memory_space=pltpu.VMEM),
        scratch_shapes=[
            pltpu.VMEM((items, half, width), jnp.bfloat16),
            pltpu.VMEM((items, half, width), jnp.bfloat16),
            pltpu.VMEM((items, half, width), jnp.bfloat16),
            pltpu.VMEM((items, 2, half, width), jnp.bfloat16),
            pltpu.VMEM((tokens, columns), jnp.float32),
            pltpu.VMEM((2, depth, width), jnp.bfloat16),
            pltpu.VMEM((2, width, columns), jnp.bfloat16),
            pltpu.SemaphoreType.DMA((2,)),
            pltpu.SemaphoreType.DMA((2,)),
        ] + [pltpu.SemaphoreType.DMA((items,))] * 6,
        compiler_params=pltpu.CompilerParams(
            collective_id=0, has_side_effects=True, vmem_limit_bytes=58 * 1024 * 1024),
        cost_estimate=pl.CostEstimate(flops=flops, transcendentals=0,
                                      bytes_accessed=2 * passes * (up_weight.size + down_weight.size)),
    )(panels, up_weight, down_weight)


def on_device(x_stored, group_units, group_order, up_weight, down_weight):
    rows, cols = lax.axis_size("row"), lax.axis_size("col")
    share = x_stored.shape[0]
    tokens = rows * share
    part = tokens // cols
    passes = 2 if part % 32 == 0 else 1
    source = unit_source(group_units, group_order)
    panels = block_scaled(x_stored.T)
    panels = lax.all_gather(panels, "col", axis=0, tiled=True)
    panels = jnp.take(panels.reshape(UNITS, BLOCK, share), source, axis=0)
    panels = lax.all_to_all(panels.reshape(rows, -1, share), "row", split_axis=0, concat_axis=0, tiled=True)
    panels = panels.transpose(0, 2, 1)
    depth = panels.shape[2]
    core = lax.rem(lax.axis_index("row"), 2)
    panels = panels.reshape(rows // 2, 2, passes, share // passes, depth)
    panels = panels.transpose(2, 1, 0, 3, 4)
    panels = jnp.where(core == 0, panels, panels[:, ::-1])
    partial = middle(panels.reshape(passes, tokens // passes, depth), up_weight, down_weight)
    partial = partial.reshape(passes, 2, rows // 2, share // passes, -1)
    partial = jnp.where(core == 0, partial, partial[:, ::-1])
    partial = partial.transpose(2, 1, 0, 3, 4).reshape(tokens, -1)
    return lax.psum_scatter(partial, "col", scatter_dimension=0, tiled=True)


def solution(mesh):
    in_specs = (P(("groups", "row"), "col"), P(), P(), P("row", "col"), P("col", "row"))
    out_specs = P(("groups", "col"), "row")
    return jax.shard_map(
        on_device, mesh=mesh, in_specs=in_specs, out_specs=out_specs, check_vma=False
    )
```

time: 470 us -> 282 us (0.60)
  waiting for transfers between devices: 315 us -> 123 us
  Pallas kernels: 0 us -> 114 us
  matrix products: 59.3 us -> 0 us
  local copies, waits for them, and re-layouts: 45.3 us -> 10.6 us
  other arithmetic: 25.5 us -> 12.1 us
    reduce_scatter x2 -> x1, waiting for transfers between devices: 186 us -> 47.6 us  [on_device(): return lax.psum_scatter(partial, 'col', scatter_dimension=0, tiled=True)]
    pallas_call x0 -> x1, Pallas kernels: none -> 114 us  [middle(): pl.pallas_call(functools.partial(middle_kernel, passes, chunks, width), o...]
    all_gather x2 -> x1, waiting for transfers between devices: 110 us -> 47.9 us  [on_device(): panels = lax.all_gather(panels, 'col', axis=0, tiled=True)]
    dot_general x2 -> x0, matrix products: 59.3 us -> none  [the longest x1 30.4 us: on_device(): jnp.dot(panels, up_weight, preferred_element_type=jnp.float32)]
    gather x1, local copies, waits for them, and re-layouts: 26.5 us -> 2.75 us  [on_device(): panels = jnp.take(panels.reshape(UNITS, BLOCK, share), source, axis=0)]
    convert_element_type x6 -> x1, other arithmetic: 20.5 us -> 2.46 us  [block_scaled(): return panels.astype(jnp.bfloat16)]
    mul x3 -> x0, local copies, waits for them, and re-layouts: 8.97 us -> none  [the longest x2 8.88 us: decode(): encoded.astype(jnp.float32).reshape(row_total, -1, BLOCK)]
    all_to_all x2 -> x1, waiting for transfers between devices: 18.7 us -> 27.6 us  [on_device(): lax.all_to_all(panels.reshape(rows, -1, share), 'row', split_axis=0, conc...]
  transfers between devices with their start and end apart: 6 -> 3, of which waited for: 5 -> 3; matrix products, arithmetic and copies ran while one was open for 5% -> 1% of each run, Pallas kernels for 0% -> 0%
where the time goes in v1:
time: 282 us; the launch traced here: 278 us
  waiting for transfers between devices  123 us (44%)
  Pallas kernels  114 us (40%)
  between operations  13.5 us (5%)
  other arithmetic  12.1 us (4%)
  local copies, waits for them, and re-layouts  10.6 us (4%)
  starting transfers between devices  4.06 us (1%)
    pallas_call x1, Pallas kernels, middle(): pl.pallas_call(functools.partial(middle_kernel, passes, chunks, width), o...  114 us
    all_gather x1, waiting for transfers between devices, on_device(): panels = lax.all_gather(panels, 'col', axis=0, tiled=True)  47.9 us
    reduce_scatter x1, waiting for transfers between devices, on_device(): return lax.psum_scatter(partial, 'col', scatter_dimension=0, tiled=True)  47.6 us
    all_to_all x1, waiting for transfers between devices, on_device(): lax.all_to_all(panels.reshape(rows, -1, share), 'row', split_axis=0, conc...  27.6 us
  transfers between devices with their start and end apart: 3, of which 3 were waited for; matrix products, arithmetic and copies ran while one was open for 1% of the time, Pallas kernels for 0%

profile of v1, /device:TPU:25, one launch (start us, length us, event | category | flops | bytes accessed | tf_op | source)
XLA Modules:
  0.0 277.9 jit_solution(5772075686340851955)
XLA Ops:
  6.5 1.4 copy.25
  8.0 0.2 convert_compare_fusion
  8.2 0.2 reduce_max.9
  8.5 2.5 fusion.1
  11.2 0.1 reduce.1
  11.3 0.2 select_reduce_fusion.3
  11.6 0.1 reduce-window.16
  11.7 0.1 reduce
  11.8 0.1 select_reduce_fusion.1
  12.0 0.2 select_reduce_fusion
  12.2 0.1 broadcast_in_dim.182
  12.3 0.1 broadcast_in_dim.183
  12.5 47.9 %all-gather.2.cloned.1.call-done = bf16[288,32,128]{2,1,0:T(8,128)(2,1)} async-done(((bf16[72,32,128]{2,1,0:T(8,128)(2,1)}), bf16[288,32,128]{2,1,0:T(8,128)(2,1)}) %all-gather.2.cloned.1.call-update) | async-done | bytes 2359312 | tf_op jit(solution)/shard_map/all_gather | solution.py:209
  60.4 2.7 gather_fusion
  63.2 3.4 %bitcast_select_fusion = bf16[4,2304,128]{2,1,0:T(8,128)(2,1)} fusion(pred[4,2304]{1,0:T(4,128)(4,1)S(1)} %broadcast_in_dim.183, bf16[4,2304,128]{2,1,0:T(8,128)(2,1)S(1)} %bitcast.24), kind=kLoop, calls=%fused_computation.3 | loop fusion | flops 1179648 | bytes 4727808 | tf_op jit(solution)/shard_map/jit(_take)/select_n | solution.py:210
  66.5 4.1 %all-to-all-start = ((bf16[4,2304,128]{2,1,0:T(8,128)(2,1)}), bf16[4,2304,128]{2,1,0:T(8,128)(2,1)S(1)}, u32[]{:S(2)}, u32[]{:S(2)}) async-start(bf16[4,2304,128]{2,1,0:T(8,128)(2,1)} %bitcast_select_fusion), calls=%async_computation | async-start | bytes 4718592 | tf_op jit(solution)/shard_map/all_to_all | solution.py:211
  70.6 27.6 %all-to-all-done = bf16[4,2304,128]{2,1,0:T(8,128)(2,1)S(1)} async-done(((bf16[4,2304,128]{2,1,0:T(8,128)(2,1)}), bf16[4,2304,128]{2,1,0:T(8,128)(2,1)S(1)}, u32[]{:S(2)}, u32[]{:S(2)}) %all-to-all-start) | async-done | bytes 2359328 | tf_op jit(solution)/shard_map/all_to_all | solution.py:211
  98.2 2.6 copy.26
  100.8 2.9 %reverse_select_fusion.1 = bf16[2,2,2,64,2304]{4,3,0,1,2:T(8,128)(2,1)S(1)} fusion(bf16[2,2,2,64,2304]{4,3,0,1,2:T(8,128)(2,1)} %bitcast.25, pred[]{:T(512)S(6)} %eq.14), kind=kLoop, calls=%fused_computation.2 | loop fusion | flops 1179648 | bytes 4718593 | tf_op jit(solution)/shard_map/jit(_where)/select_n | solution.py:217
  103.8 1.6 copy.27
  105.3 114.4 %shard_map.55 = bf16[2,256,2304]{2,1,0:T(8,128)(2,1)} custom-call(bf16[2,256,2304]{2,1,0:T(8,128)(2,1)} %bitcast.26, bf16[2304,9216]{1,0:T(8,128)(2,1)} %up_ref.1, bf16[9216,2304]{1,0:T(8,128)(2,1)} %down_ref.1), custom_call_target="tpu_custom_call" | custom-call | flops 43486543872 | bytes 169869312 | tf_op jit(solution)/shard_map/pallas_call | solution.py:177
  219.7 1.8 copy.29
  221.6 1.8 reverse_select_fusion
  223.4 47.6 %reduce-scatter.2.cloned.1.call-done = bf16[128,2304]{1,0:T(8,128)(2,1)} async-done(((bf16[512,2304]{1,0:T(8,128)(2,1)}), bf16[128,2304]{1,0:T(8,128)(2,1)}) %reduce-scatter.2.cloned.1.call-update) | async-done | bytes 589840 | tf_op jit(solution)/shard_map/reduce_scatter | solution.py:222
  (19 shorter events, 0.6 us)
Async XLA Ops:
  6.5 53.9 %all-gather.2.cloned.1.call-start = ((), (), s32[]{:S(2)}) async-start(), calls=%async_computation.2 | async-start | bytes 2949120 | tf_op jit(solution)/shard_map/all_gather | solution.py:209
  8.5 2.5 copy-start
  8.5 2.8 %copy-start.1 = (s32[64]{0:T(128)S(1)}, s32[64]{0:T(128)}, u32[]{:S(2)}) copy-start(s32[64]{0:T(128)} %param.7) | copy-start | bytes 772
  66.5 31.7 %all-to-all-start = ((bf16[4,2304,128]{2,1,0:T(8,128)(2,1)}), bf16[4,2304,128]{2,1,0:T(8,128)(2,1)S(1)}, u32[]{:S(2)}, u32[]{:S(2)}) async-start(bf16[4,2304,128]{2,1,0:T(8,128)(2,1)} %bitcast_select_fusion), calls=%async_computation | async-start | bytes 4718592 | tf_op jit(solution)/shard_map/all_to_all | solution.py:211
  70.6 200.4 %reduce-scatter.2.cloned.1.call-start = ((), (), s32[]{:S(2)}) async-start(), calls=%async_computation.3 | async-start | bytes 2949120 | tf_op jit(solution)/shard_map/reduce_scatter | solution.py:222
Sparse Core Ops, SparseCore 0:
  11.1 49.2 all-gather.1
  223.5 47.4 reduce-scatter.1

commit v2 on v1

v2 whole, which is shorter than its diff:
```python
import functools
import jax
import jax.numpy as jnp
from jax import lax
from jax.experimental import pallas as pl
from jax.experimental.pallas import tpu as pltpu
from jax.sharding import PartitionSpec as P

BLOCK = 32
UNITS = 288
MESH = pl.DeviceIdType.MESH
LAG = 5
NEAR = 4


def unit_source(group_units, group_order):
    count = group_units.shape[0]
    group_ids = jnp.arange(count, dtype=jnp.int32)
    onehot = (group_order[:, None] == group_ids[None, :]).astype(jnp.int32)
    canon_start = jnp.cumsum(group_units) - group_units
    slot_length = jnp.sum(onehot * group_units[None, :], axis=1)
    slot_canon = jnp.sum(onehot * canon_start[None, :], axis=1)
    slot_start = jnp.cumsum(slot_length) - slot_length
    unit_ids = jnp.arange(UNITS, dtype=jnp.int32)
    inside = (unit_ids[:, None] >= slot_start[None, :]) & (
        unit_ids[:, None] < (slot_start + slot_length)[None, :]
    )
    canon_unit = jnp.sum(
        jnp.where(inside, slot_canon[None, :] + unit_ids[:, None] - slot_start[None, :], 0), axis=1
    )
    source = jnp.sum(
        jnp.where(canon_unit[None, :] == unit_ids[:, None], unit_ids[None, :], 0), axis=1
    )
    return source


def exponent_floor(magnitude, lowest, highest, offset):
    result = jnp.full(magnitude.shape, 2.0 ** (lowest + offset), jnp.float32)
    for power in range(lowest + 1, highest + 1):
        result = jnp.where(magnitude >= 2.0**power, jnp.float32(2.0 ** (power + offset)), result)
    return result


def block_scaled(values):
    features, tokens = values.shape
    blocks = values.astype(jnp.float32).reshape(features // BLOCK, BLOCK, tokens)
    largest = jnp.max(jnp.abs(blocks), axis=1)
    scale = exponent_floor(largest, -20, 8, -8)[:, None, :]
    magnitude = jnp.abs(blocks) / scale
    spacing = exponent_floor(magnitude, -6, 8, -3)
    level = jnp.minimum(jnp.floor(magnitude / spacing + 0.5) * spacing, 448.0)
    panels = jnp.where(blocks < 0.0, -level, level) * scale
    return panels.astype(jnp.bfloat16)


def layer_kernel(passes, chunks, width, *refs):
    place_ref, lane_ref, x_ref, up_ref, down_ref, out_ref = refs[:6]
    gather = refs[6:6 + passes]
    (moved, blocks, panel, near, mine, hand, far, hid, total, own, parts, up_buf, down_buf,
     keep_sem, gather_send, gather_recv, moved_send, moved_recv, up_sem, down_sem, near_send, near_recv,
     far_send, far_recv, hid_send, hid_recv, part_send, part_recv) = refs[6 + passes:]
    items = passes * chunks
    half = hand.shape[1]
    cols, seg = own.shape[1], own.shape[2]
    units, lanes = blocks.shape[2], blocks.shape[4]
    local = x_ref.shape[1]
    piece = lanes // passes
    columns = out_ref.shape[1]
    row, col = lax.axis_index("row"), lax.axis_index("col")
    core = lax.rem(row, 2)
    sibling = row + 1 - 2 * core
    partner = lax.rem(row + 2, 4)
    across = lax.rem(sibling + 2, 4)

    barrier = pltpu.get_barrier_semaphore()
    for other in (sibling, partner, across):
        pl.semaphore_signal(barrier, inc=1, device_id={"row": other}, device_id_type=MESH)
    for k in range(1, cols):
        pl.semaphore_signal(barrier, inc=1, device_id={"col": lax.rem(col + k, cols)}, device_id_type=MESH)

    def keep(p):
        return pltpu.make_async_copy(x_ref.at[p], gather[p].at[pl.ds(col * local, local)], keep_sem.at[p])

    def to_col(p, k):
        return pltpu.make_async_remote_copy(
            src_ref=x_ref.at[p], dst_ref=gather[p].at[pl.ds(col * local, local)], send_sem=gather_send.at[p, k],
            recv_sem=gather_recv.at[p, k], device_id={"col": lax.rem(col + k, cols)}, device_id_type=MESH)

    def to_row(p, k):
        target = (row, partner, across, sibling)[k]
        return pltpu.make_async_remote_copy(
            src_ref=moved.at[p, k - 1], dst_ref=blocks.at[p, k], send_sem=moved_send.at[p, k - 1],
            recv_sem=moved_recv.at[p, k - 1], device_id={"row": target}, device_id_type=MESH)

    def up_copy(item):
        slot = lax.rem(item, 2)
        chunk = pl.ds(pl.multiple_of(lax.rem(item, chunks) * width, width), width)
        return pltpu.make_async_copy(up_ref.at[:, chunk], up_buf.at[slot], up_sem.at[slot])

    def down_copy(item):
        slot = lax.rem(item, 2)
        chunk = pl.ds(pl.multiple_of(lax.rem(item, chunks) * width, width), width)
        return pltpu.make_async_copy(down_ref.at[chunk, :], down_buf.at[slot], down_sem.at[slot])

    def to_near(item):
        slot = lax.rem(item, NEAR)
        return pltpu.make_async_remote_copy(
            src_ref=near.at[slot], dst_ref=hand.at[item], send_sem=near_send.at[slot],
            recv_sem=near_recv.at[item], device_id={"row": sibling}, device_id_type=MESH)

    def to_far(item):
        return pltpu.make_async_remote_copy(
            src_ref=far.at[item], dst_ref=hid.at[item, 0], send_sem=far_send.at[item],
            recv_sem=far_recv.at[item], device_id={"row": partner}, device_id_type=MESH)

    def to_hid(item):
        return pltpu.make_async_remote_copy(
            src_ref=hid.at[item, 0], dst_ref=hid.at[item, 1], send_sem=hid_send.at[item],
            recv_sem=hid_recv.at[item], device_id={"row": sibling}, device_id_type=MESH)

    def to_part(p, k):
        return pltpu.make_async_remote_copy(
            src_ref=own.at[p, k], dst_ref=parts.at[p, k], send_sem=part_send.at[p, k],
            recv_sem=part_recv.at[p, k], device_id={"col": lax.rem(col + k, cols)}, device_id_type=MESH)

    up_copy(0).start()
    up_copy(1).start()
    down_copy(0).start()
    down_copy(1).start()
    for p in range(passes):
        keep(p).start()
    pl.semaphore_wait(barrier, cols + 2)
    for p in range(passes):
        for k in range(1, cols):
            to_col(p, k).start()

    lane = lax.broadcasted_iota(jnp.int32, (BLOCK, lanes), 1)

    def move(p):
        for k in (1, 2, 3, 0):
            target = (row, partner, across, sibling)[k]

            def one(v, carry):
                first = target * (units * passes) + v
                result = gather[p][place_ref[first]]
                if passes == 2:
                    second = first + units
                    a = result.astype(jnp.float32)
                    b = gather[p][place_ref[second]].astype(jnp.float32)
                    a = jnp.where(lane_ref[first] == 0, a, pltpu.roll(a, piece, 1))
                    b = jnp.where(lane_ref[second] == 1, b, pltpu.roll(b, piece, 1))
                    result = jnp.where(lane < piece, a, b).astype(jnp.bfloat16)
                if k == 0:
                    blocks[p, 0, v] = result
                else:
                    moved[p, k - 1, v] = result
                return carry

            lax.fori_loop(0, units, one, 0, unroll=4)
            if k > 0:
                to_row(p, k).start()

    def lay(p):
        for k in range(4):
            origin = (row, partner, across, sibling)[k]
            at = (half if k >= 2 else 0) + lax.div(origin, 2) * piece

            def one(j, carry):
                tile = blocks[p, k, pl.ds(4 * j, 4)].reshape(4 * BLOCK, lanes).T
                for q in range(passes):
                    chunk = pl.ds(pl.multiple_of(q * units * BLOCK + 4 * BLOCK * j, 128), 4 * BLOCK)
                    panel[p, pl.ds(pl.multiple_of(at, piece), piece), chunk] = tile[q * piece:(q + 1) * piece]
                return carry

            lax.fori_loop(0, units // 4, one, 0)

    for p in range(passes):
        keep(p).wait()
        for k in range(1, cols):
            to_col(p, k).wait_recv()
        move(p)
    for k in (1, 2, 3):
        to_row(0, k).wait_recv()
    lay(0)

    def step(t, carry):
        for p in range(1, passes):
            @pl.when(t == p * chunks)
            def _():
                for k in (1, 2, 3):
                    to_row(p, k).wait_recv()
                lay(p)

        @pl.when(t < items)
        def _():
            up_copy(t).wait()
            slot = lax.rem(t, 2)

            @pl.when(t >= NEAR)
            def _():
                to_near(t - NEAR).wait_send()

            product = jnp.dot(panel[lax.div(t, chunks)], up_buf[slot], preferred_element_type=jnp.float32)
            near[lax.rem(t, NEAR)] = product[half:].astype(jnp.bfloat16)
            to_near(t).start()
            mine[slot] = product[:half]

            @pl.when(t + 2 < items)
            def _():
                up_copy(t + 2).start()

        @pl.when((t >= 1) & (t < items + 1))
        def _():
            item = t - 1
            to_near(item).wait_recv()
            far[item] = (mine[lax.rem(item, 2)] + hand[item].astype(jnp.float32)).astype(jnp.bfloat16)
            to_far(item).start()

        @pl.when((t >= LAG) & (t < items + LAG))
        def _():
            item = t - LAG
            to_far(item).wait_recv()
            summed = far[item].astype(jnp.float32) + hid[item, 0].astype(jnp.float32)
            hid[item, 0] = jnp.square(jnp.maximum(summed, 0.0)).astype(jnp.bfloat16)
            to_hid(item).start()

        @pl.when(t >= LAG + 1)
        def _():
            item = t - LAG - 1
            slot = lax.rem(item, 2)
            place = lax.rem(item, chunks)
            to_hid(item).wait_recv()
            down_copy(item).wait()
            hidden = hid[item].reshape(2 * half, width)
            tile = columns // 3
            for n in range(3):
                at = slice(n * tile, (n + 1) * tile)
                product = jnp.dot(hidden, down_buf[slot, :, at], preferred_element_type=jnp.float32)
                total[:, at] = jnp.where(place == 0, product, total[:, at] + product)

            @pl.when(item + 2 < items)
            def _():
                down_copy(item + 2).start()

            @pl.when(place == chunks - 1)
            def _():
                p = lax.div(item, chunks)
                for k in (*range(1, cols), 0):
                    target = lax.rem(col + k, cols)
                    origin = lax.div(target, piece // seg)
                    at = (lax.rem(origin + core, 2) * half + lax.div(origin, 2) * piece
                          + lax.rem(target, piece // seg) * seg)
                    own[p, k] = total[pl.ds(pl.multiple_of(at, seg), seg), :].astype(jnp.bfloat16)
                    if k > 0:
                        to_part(p, k).start()

        return carry

    lax.fori_loop(0, items + LAG + 1, step, 0)

    def drain(item, carry):
        to_far(item).wait_send()
        to_hid(item).wait_send()
        return carry

    lax.fori_loop(0, items, drain, 0)
    for item in range(max(items - NEAR, 0), items):
        to_near(item).wait_send()
    for p in range(passes):
        for k in range(1, cols):
            to_col(p, k).wait_send()
        for k in (1, 2, 3):
            to_row(p, k).wait_send()
    for p in range(passes):
        mixed = own[p, 0].astype(jnp.float32)
        for k in range(1, cols):
            to_part(p, k).wait_recv()
            mixed = mixed + parts[p, k].astype(jnp.float32)
        out_ref[p * seg:(p + 1) * seg, :] = mixed.astype(jnp.bfloat16)
    for p in range(passes):
        for k in range(1, cols):
            to_part(p, k).wait_send()


def layer(cols, place, lane, packed, up_weight, down_weight):
    passes, local_units, _, lanes = packed.shape
    depth, hidden = up_weight.shape
    columns = down_weight.shape[1]
    tokens = 4 * lanes // passes
    units = depth // BLOCK // passes
    width = next(w for w in (512, 384, 256, 128) if hidden % w == 0)
    chunks = hidden // width
    items = passes * chunks
    half = tokens // 2
    seg = tokens // cols
    flops = 2 * passes * tokens * hidden * (depth + columns)
    vmem = pl.BlockSpec(memory_space=pltpu.VMEM)
    smem = pl.BlockSpec(memory_space=pltpu.SMEM)
    hbm = pl.BlockSpec(memory_space=pl.ANY)
    dma = pltpu.SemaphoreType.DMA
    return pl.pallas_call(
        functools.partial(layer_kernel, passes, chunks, width),
        out_shape=jax.ShapeDtypeStruct((passes * seg, columns), jnp.bfloat16),
        in_specs=[smem, smem, vmem, hbm, hbm],
        out_specs=vmem,
        scratch_shapes=[pltpu.VMEM((cols * local_units, BLOCK, lanes), jnp.bfloat16)] * passes + [
            pltpu.VMEM((passes, 3, units, BLOCK, lanes), jnp.bfloat16),
            pltpu.VMEM((passes, 4, units, BLOCK, lanes), jnp.bfloat16),
            pltpu.VMEM((passes, tokens, depth), jnp.bfloat16),
            pltpu.VMEM((NEAR, half, width), jnp.bfloat16),
            pltpu.VMEM((2, half, width), jnp.float32),
            pltpu.VMEM((items, half, width), jnp.bfloat16),
            pltpu.VMEM((items, half, width), jnp.bfloat16),
            pltpu.VMEM((items, 2, half, width), jnp.bfloat16),
            pltpu.VMEM((tokens, columns), jnp.float32),
            pltpu.VMEM((passes, cols, seg, columns), jnp.bfloat16),
            pltpu.VMEM((passes, cols, seg, columns), jnp.bfloat16),
            pltpu.VMEM((2, depth, width), jnp.bfloat16),
            pltpu.VMEM((2, width, columns), jnp.bfloat16),
            dma((passes,)), dma((passes, cols)), dma((passes, cols)), dma((passes, 3)), dma((passes, 3)),
            dma((2,)), dma((2,)), dma((NEAR,)), dma((items,)), dma((items,)), dma((items,)),
            dma((items,)), dma((items,)), dma((passes, cols)), dma((passes, cols)),
        ],
        compiler_params=pltpu.CompilerParams(
            collective_id=0, has_side_effects=True, vmem_limit_bytes=60 * 1024 * 1024),
        cost_estimate=pl.CostEstimate(flops=flops, transcendentals=0,
                                      bytes_accessed=2 * passes * (up_weight.size + down_weight.size)),
    )(place, lane, packed, up_weight, down_weight)


def on_device(x_stored, group_units, group_order, up_weight, down_weight):
    rows, cols = lax.axis_size("row"), lax.axis_size("col")
    share, features = x_stored.shape
    passes = 2 if rows == cols else 1
    units = features // BLOCK // passes
    piece = share // passes
    packed = x_stored.reshape(passes, piece, passes, units, BLOCK).transpose(0, 3, 4, 2, 1)
    packed = block_scaled(packed.reshape(passes * units * BLOCK, share)).reshape(passes, units, BLOCK, share)
    source = unit_source(group_units, group_order)
    origin, inside = source // (units * passes), source % (units * passes)
    return layer(cols, origin * units + inside % units, inside // units, packed, up_weight, down_weight)


def solution(mesh):
    in_specs = (P(("groups", "row"), "col"), P(), P(), P("row", "col"), P("col", "row"))
    out_specs = P(("groups", "col"), "row")
    return jax.shard_map(
        on_device, mesh=mesh, in_specs=in_specs, out_specs=out_specs, check_vma=False
    )
```

time: 282 us -> 229 us (0.81); the launches traced: 278 us -> 229 us
  waiting for transfers between devices: 123 us -> 0 us
  Pallas kernels: 114 us -> 204 us
  between operations: 13.5 us -> 0.29 us
  local copies, waits for them, and re-layouts: 10.6 us -> 16.4 us
  starting transfers between devices: 4.06 us -> 0 us
  other arithmetic: 12.1 us -> 8.9 us
    pallas_call x1, Pallas kernels: 114 us -> 204 us  [layer(): pl.pallas_call(functools.partial(layer_kernel, passes, chunks, width), ou...]
    all_gather x1 -> x0, waiting for transfers between devices: 47.9 us -> none  [on_device(): panels = lax.all_gather(panels, 'col', axis=0, tiled=True)]
    reduce_scatter x1 -> x0, waiting for transfers between devices: 47.6 us -> none  [on_device(): return lax.psum_scatter(partial, 'col', scatter_dimension=0, tiled=True)]
    all_to_all x1 -> x0, waiting for transfers between devices: 27.6 us -> none  [on_device(): lax.all_to_all(panels.reshape(rows, -1, share), 'row', split_axis=0, conc...]
    abs x0 -> x4, local copies, waits for them, and re-layouts: none -> 8.15 us  [block_scaled(): magnitude = jnp.abs(blocks) / scale]
    select_n x4 -> x1, other arithmetic: 8.14 us -> 0.63 us  [on_device(): inside // units]
    lt x0 -> x4, local copies, waits for them, and re-layouts: none -> 4.13 us  [block_scaled(): panels = jnp.where(blocks < 0.0, -level, level) * scale]
    all_to_all x1 -> x0, starting transfers between devices: 4.05 us -> none  [on_device(): lax.all_to_all(panels.reshape(rows, -1, share), 'row', split_axis=0, conc...]
  transfers between devices with their start and end apart: 3 -> 0, of which waited for: 3 -> 0; matrix products, arithmetic and copies ran while one was open for 1% -> 0% of each run, Pallas kernels for 0% -> 0%
where the time goes in v2:
time: 229 us
  Pallas kernels  204 us (89%)
  local copies, waits for them, and re-layouts  16.4 us (7%)
  other arithmetic  8.9 us (4%)
    pallas_call x1, Pallas kernels, layer(): pl.pallas_call(functools.partial(layer_kernel, passes, chunks, width), ou...  204 us
    abs x4, local copies, waits for them, and re-layouts, block_scaled(): magnitude = jnp.abs(blocks) / scale  8.15 us

profile of v2, /device:TPU:25, one launch (start us, length us, event | category | flops | bytes accessed | tf_op | source)
XLA Modules:
  0.0 229.1 jit_solution(12327804602098565158)
XLA Ops:
  0.0 1.2 convert_abs_fusion
  1.2 0.4 copy.55
  1.5 1.3 abs.18
  2.8 2.1 reduce_max.9
  5.0 0.5 compare_bitcast_fusion
  7.4 0.3 bitcast_select_fusion.2
  7.8 0.1 reshape.312
  7.9 0.7 select_select_fusion
  8.5 3.7 %copy.56 = f32[2,36,32,2,64]{4,3,2,1,0:T(2,128)} copy(f32[2,36,32,2,64]{4,0,2,1,3:T(2,128)S(1)} %bitcast.54) | data formatting | bytes 2359296 | tf_op jit(solution)/shard_map/abs | solution.py:49
  12.2 2.8 %abs.20 = f32[2,36,32,128]{3,2,1,0:T(8,128)S(1)} reshape(f32[2,36,32,2,64]{4,3,2,1,0:T(2,128)} %copy.56) | data formatting | bytes 2359296 | tf_op jit(solution)/shard_map/abs | solution.py:49
  15.0 0.2 convert_compare_fusion
  15.2 0.5 copy.53
  15.7 0.9 lt.43
  16.7 1.7 copy.54
  18.4 1.0 lt.45
  19.4 2.4 %fusion.1.refs_2_ = bf16[2,36,32,128]{3,2,1,0:T(8,128)(2,1)} fusion(pred[2,36,32,128]{3,2,1,0:T(8,128)(4,1)S(1)} %lt.45, f32[2,36,32,128]{3,2,1,0:T(8,128)S(1)} %abs.20, f32[2,36,128]{2,1,0:T(8,128)S(1)} %copy-done.1), kind=kLoop, calls=%fused_computation.4 | loop fusion | flops 11501568 | bytes 2101248 | tf_op jit(solution)/shard_map/convert_element_type | solution.py:53
  22.1 0.1 reduce.3
  22.2 0.2 select_reduce_fusion.3
  22.6 0.1 reduce.2
  22.7 0.1 select_reduce_fusion.1
  22.8 0.2 select_reduce_fusion
  23.0 0.6 add_select_fusion
  23.6 203.6 %shard_map.55 = bf16[128,2304]{1,0:T(8,128)(2,1)} custom-call(s32[288]{0:T(512)} %get-tuple-element.21.refs_0_, s32[288]{0:T(512)} %get-tuple-element.20.refs_1_, bf16[2,36,32,128]{3,2,1,0:T(8,128)(2,1)} %fusion.1.refs_2_, bf16[2304,9216]{1,0:T(8,128)(2,1)} %refs_3_.1, bf16[9216,2304]{1,0:T(8,128)(2,1)} %refs_4_.1), custom_call_target="tpu_custom_call" | custom-call | flops 43486543872 | bytes 169869312 | tf_op jit(solution)/shard_map/pallas_call | solution.py:301
  227.2 1.9 copy.75
  (41 shorter events, 2.3 us)
Async XLA Ops:
  12.2 2.8 %copy-start = (bf16[128,2304]{1,0:T(8,128)(2,1)S(1)}, bf16[128,2304]{1,0:T(8,128)(2,1)}, u32[]{:S(2)}) copy-start(bf16[128,2304]{1,0:T(8,128)(2,1)} %param.5) | copy-start | bytes 1769476
  18.4 1.0 copy-start.1
  19.4 2.5 %copy-start.2 = (s32[64]{0:T(128)S(1)}, s32[64]{0:T(128)}, u32[]{:S(2)}) copy-start(s32[64]{0:T(128)} %param.6) | copy-start | bytes 772
  19.4 2.8 %copy-start.3 = (s32[64]{0:T(128)S(1)}, s32[64]{0:T(128)}, u32[]{:S(2)}) copy-start(s32[64]{0:T(128)} %param.7) | copy-start | bytes 772

commit v3 on v2

--- a/solution.py
+++ b/solution.py
@@ -53,11 +53,29 @@
     return panels.astype(jnp.bfloat16)
 
 
+def tile_scaled(values):
+    blocks = values.reshape(-1, BLOCK, values.shape[1])
+    size = jnp.abs(blocks)
+    largest = jnp.max(size, axis=1, keepdims=True)
+    scale = jnp.full(largest.shape, 2.0**-28, jnp.float32)
+    inverse = jnp.full(largest.shape, 2.0**28, jnp.float32)
+    for power in range(-19, 9):
+        above = largest >= 2.0**power
+        scale = jnp.where(above, jnp.float32(2.0 ** (power - 8)), scale)
+        inverse = jnp.where(above, jnp.float32(2.0 ** (8 - power)), inverse)
+    size = size * inverse
+    nudged = size * (1.0 + 2.0**-12)
+    wide = nudged * (2.0**20 + 1.0)
+    level = jnp.where(size < 2.0**-6, jnp.floor(size * 512.0 + 0.5) * (1.0 / 512.0), wide - (wide - nudged))
+    level = jnp.minimum(level, 448.0) * scale
+    return jnp.where(blocks < 0.0, -level, level)
+
+
 def layer_kernel(passes, chunks, width, *refs):
-    place_ref, lane_ref, x_ref, up_ref, down_ref, out_ref = refs[:6]
+    place_ref, lane_ref, raw_ref, up_ref, down_ref, out_ref = refs[:6]
     gather = refs[6:6 + passes]
-    (moved, blocks, panel, near, mine, hand, far, hid, total, own, parts, up_buf, down_buf,
-     keep_sem, gather_send, gather_recv, moved_send, moved_recv, up_sem, down_sem, near_send, near_recv,
+    (x_ref, moved, blocks, panel, near, mine, hand, far, hid, total, own, parts, up_buf, down_buf,
+     keep_sem, gather_send, gather_recv, moved_send, moved_recv, relay_send, relay_recv, up_sem, down_sem, near_send, near_recv,
      far_send, far_recv, hid_send, hid_recv, part_send, part_recv) = refs[6 + passes:]
     items = passes * chunks
     half = hand.shape[1]
@@ -68,6 +86,10 @@
     columns = out_ref.shape[1]
     row, col = lax.axis_index("row"), lax.axis_index("col")
     core = lax.rem(row, 2)
+    relay = units % cols == 0
+    count = units // cols if relay else units
+    first_unit = col * count if relay else 0
+    part = pl.ds(first_unit, count)
     sibling = row + 1 - 2 * core
     partner = lax.rem(row + 2, 4)
     across = lax.rem(sibling + 2, 4)
@@ -88,9 +110,15 @@
 
     def to_row(p, k):
         target = (row, partner, across, sibling)[k]
-        return pltpu.make_async_remote_copy(
-            src_ref=moved.at[p, k - 1], dst_ref=blocks.at[p, k], send_sem=moved_send.at[p, k - 1],
+        mine_of = slice(None) if k == 3 else part
+        return pltpu.make_async_remote_copy(
+            src_ref=moved.at[p, k - 1, mine_of], dst_ref=blocks.at[p, k, mine_of], send_sem=moved_send.at[p, k - 1],
             recv_sem=moved_recv.at[p, k - 1], device_id={"row": target}, device_id_type=MESH)
+
+    def to_relay(p, k, m):
+        return pltpu.make_async_remote_copy(
+            src_ref=blocks.at[p, k, part], dst_ref=blocks.at[p, k, part], send_sem=relay_send.at[p, k - 1, m],
+            recv_sem=relay_recv.at[p, k - 1, m], device_id={"col": lax.rem(col + m, cols)}, device_id_type=MESH)
 
     def up_copy(item):
         slot = lax.rem(item, 2)
@@ -127,12 +155,34 @@
     up_copy(1).start()
     down_copy(0).start()
     down_copy(1).start()
+
+    if raw_ref.ndim == 4:
+        x_ref[...] = raw_ref[...]
+    else:
+        wide_lane = lax.broadcasted_iota(jnp.int32, (4 * BLOCK, lanes), 1)
+
+        def encode(j, carry):
+            def tile(q):
+                chunk = pl.ds(pl.multiple_of(q * units * BLOCK + 4 * BLOCK * j, 128), 4 * BLOCK)
+                return tile_scaled(raw_ref[:, chunk].astype(jnp.float32).T).reshape(4 * BLOCK, lanes)
+
+            if passes == 1:
+                packed = [tile(0)]
+            else:
+                a, b = tile(0), tile(1)
+                packed = [jnp.where(wide_lane < piece, a, pltpu.roll(b, piece, 1)),
+                          jnp.where(wide_lane < piece, pltpu.roll(a, piece, 1), b)]
+            for p in range(passes):
+                x_ref[p, pl.ds(4 * j, 4)] = packed[p].astype(jnp.bfloat16).reshape(4, BLOCK, lanes)
+            return carry
+
+        lax.fori_loop(0, local // 4, encode, 0)
+
     for p in range(passes):
         keep(p).start()
     pl.semaphore_wait(barrier, cols + 2)
-    for p in range(passes):
-        for k in range(1, cols):
-            to_col(p, k).start()
+    for k in range(1, cols):
+        to_col(0, k).start()
 
     lane = lax.broadcasted_iota(jnp.int32, (BLOCK, lanes), 1)
 
@@ -140,7 +190,10 @@
         for k in (1, 2, 3, 0):
             target = (row, partner, across, sibling)[k]
 
-            def one(v, carry):
+            begin, length = (first_unit, count) if k in (1, 2) else (0, units)
+
+            def one(step_of, carry):
+                v = begin + step_of
                 first = target * (units * passes) + v
                 result = gather[p][place_ref[first]]
                 if passes == 2:
@@ -156,7 +209,7 @@
                     moved[p, k - 1, v] = result
                 return carry
 
-            lax.fori_loop(0, units, one, 0, unroll=4)
+            lax.fori_loop(0, length, one, 0, unroll=4 if length % 4 == 0 else 3)
             if k > 0:
                 to_row(p, k).start()
 
@@ -174,22 +227,40 @@
 
             lax.fori_loop(0, units // 4, one, 0)
 
-    for p in range(passes):
+    def collect(p):
         keep(p).wait()
         for k in range(1, cols):
             to_col(p, k).wait_recv()
         move(p)
-    for k in (1, 2, 3):
-        to_row(0, k).wait_recv()
-    lay(0)
+
+    def hand_on(p):
+        for k in (1, 2):
+            to_row(p, k).wait_recv()
+            if relay:
+                for m in range(1, cols):
+                    to_relay(p, k, m).start()
+
+    def finish(p):
+        to_row(p, 3).wait_recv()
+        if relay:
+            for k in (1, 2):
+                for m in range(1, cols):
+                    to_relay(p, k, m).wait_recv()
+        lay(p)
+
+    collect(0)
+    hand_on(0)
+    for p in range(1, passes):
+        for k in range(1, cols):
+            to_col(p, k).start()
+    finish(0)
 
     def step(t, carry):
         for p in range(1, passes):
-            @pl.when(t == p * chunks)
-            def _():
-                for k in (1, 2, 3):
-                    to_row(p, k).wait_recv()
-                lay(p)
+            begin = (p - 1) * chunks + chunks // 2
+            pl.when(t == begin)(functools.partial(collect, p))
+            pl.when(t == begin + 3)(functools.partial(hand_on, p))
+            pl.when(t == p * chunks)(functools.partial(finish, p))
 
         @pl.when(t < items)
         def _():
@@ -271,6 +342,10 @@
             to_col(p, k).wait_send()
         for k in (1, 2, 3):
             to_row(p, k).wait_send()
+        if relay:
+            for k in (1, 2):
+                for m in range(1, cols):
+                    to_relay(p, k, m).wait_send()
     for p in range(passes):
         mixed = own[p, 0].astype(jnp.float32)
         for k in range(1, cols):
@@ -282,8 +357,11 @@
             to_part(p, k).wait_send()
 
 
-def layer(cols, place, lane, packed, up_weight, down_weight):
-    passes, local_units, _, lanes = packed.shape
+def layer(cols, passes, place, lane, values, up_weight, down_weight):
+    if values.ndim == 4:
+        local_units, lanes = values.shape[1], values.shape[3]
+    else:
+        local_units, lanes = values.shape[1] // BLOCK // passes, values.shape[0]
     depth, hidden = up_weight.shape
     columns = down_weight.shape[1]
     tokens = 4 * lanes // passes
@@ -304,6 +382,7 @@
         in_specs=[smem, smem, vmem, hbm, hbm],
         out_specs=vmem,
         scratch_shapes=[pltpu.VMEM((cols * local_units, BLOCK, lanes), jnp.bfloat16)] * passes + [
+            pltpu.VMEM((passes, local_units, BLOCK, lanes), jnp.bfloat16),
             pltpu.VMEM((passes, 3, units, BLOCK, lanes), jnp.bfloat16),
             pltpu.VMEM((passes, 4, units, BLOCK, lanes), jnp.bfloat16),
             pltpu.VMEM((passes, tokens, depth), jnp.bfloat16),
@@ -318,6 +397,7 @@
             pltpu.VMEM((2, depth, width), jnp.bfloat16),
             pltpu.VMEM((2, width, columns), jnp.bfloat16),
             dma((passes,)), dma((passes, cols)), dma((passes, cols)), dma((passes, 3)), dma((passes, 3)),
+            dma((passes, 2, cols)), dma((passes, 2, cols)),
             dma((2,)), dma((2,)), dma((NEAR,)), dma((items,)), dma((items,)), dma((items,)),
             dma((items,)), dma((items,)), dma((passes, cols)), dma((passes, cols)),
         ],
@@ -325,7 +405,7 @@
             collective_id=0, has_side_effects=True, vmem_limit_bytes=60 * 1024 * 1024),
         cost_estimate=pl.CostEstimate(flops=flops, transcendentals=0,
                                       bytes_accessed=2 * passes * (up_weight.size + down_weight.size)),
-    )(place, lane, packed, up_weight, down_weight)
+    )(place, lane, values, up_weight, down_weight)
 
 
 def on_device(x_stored, group_units, group_order, up_weight, down_weight):
@@ -334,11 +414,14 @@
     passes = 2 if rows == cols else 1
     units = features // BLOCK // passes
     piece = share // passes
-    packed = x_stored.reshape(passes, piece, passes, units, BLOCK).transpose(0, 3, 4, 2, 1)
-    packed = block_scaled(packed.reshape(passes * units * BLOCK, share)).reshape(passes, units, BLOCK, share)
+    values = x_stored
+    if features % (128 * passes) != 0:
+        packed = x_stored.reshape(passes, piece, passes, units, BLOCK).transpose(0, 3, 4, 2, 1)
+        packed = block_scaled(packed.reshape(passes * units * BLOCK, share))
+        values = packed.reshape(passes, units, BLOCK, share)
     source = unit_source(group_units, group_order)
     origin, inside = source // (units * passes), source % (units * passes)
-    return layer(cols, origin * units + inside % units, inside // units, packed, up_weight, down_weight)
+    return layer(cols, passes, origin * units + inside % units, inside // units, values, up_weight, down_weight)
 
 
 def solution(mesh):

time: 229 us -> 199 us (0.87)
  local copies, waits for them, and re-layouts: 16.4 us -> 2.76 us
  Pallas kernels: 204 us -> 192 us
  other arithmetic: 8.9 us -> 2.84 us
    pallas_call x1, Pallas kernels: 204 us -> 192 us  [layer(): pl.pallas_call(functools.partial(layer_kernel, passes, chunks, width), ou...]
    abs x4 -> x0, local copies, waits for them, and re-layouts: 8.15 us -> none  [block_scaled(): magnitude = jnp.abs(blocks) / scale]
    lt x4 -> x0, local copies, waits for them, and re-layouts: 4.13 us -> none  [block_scaled(): panels = jnp.where(blocks < 0.0, -level, level) * scale]
    convert_element_type x1 -> x0, other arithmetic: 2.45 us -> none  [block_scaled(): return panels.astype(jnp.bfloat16)]
where the time goes in v3:
time: 199 us; the launch traced here: 197 us
  Pallas kernels  192 us (96%)
  other arithmetic  2.84 us (1%)
  local copies, waits for them, and re-layouts  2.76 us (1%)
    pallas_call x1, Pallas kernels, layer(): pl.pallas_call(functools.partial(layer_kernel, passes, chunks, width), ou...  192 us

profile of v3, /device:TPU:25, one launch (start us, length us, event | category | flops | bytes accessed | tf_op | source)
XLA Modules:
  0.0 197.4 jit_solution(5651018507274038285)
XLA Ops:
  0.0 0.7 copy.11
  0.7 0.1 reduce-window.17
  0.8 0.1 reduce.1
  0.9 0.7 sub.27
  1.6 0.8 select_reduce_fusion.3
  2.5 0.1 copy.10
  2.6 0.1 reduce-window.16
  2.7 0.1 reduce
  2.8 0.1 select_reduce_fusion.1
  2.9 0.2 select_reduce_fusion
  3.1 0.6 add_select_fusion
  3.7 191.7 %shard_map.55 = bf16[128,2304]{1,0:T(8,128)(2,1)} custom-call(s32[288]{0:T(512)} %get-tuple-element.8.refs_0_, s32[288]{0:T(512)} %get-tuple-element.7.refs_1_, bf16[128,2304]{1,0:T(8,128)(2,1)} %refs_2_.1, bf16[2304,9216]{1,0:T(8,128)(2,1)} %refs_3_.1, bf16[9216,2304]{1,0:T(8,128)(2,1)} %refs_4_.1), custom_call_target="tpu_custom_call" | custom-call | flops 43486543872 | bytes 169869312 | tf_op jit(solution)/shard_map/pallas_call | solution.py:379
  195.4 1.9 copy.13
  (1 shorter events, 0.0 us)

commit v4 on v3

--- a/solution.py
+++ b/solution.py
@@ -9,7 +9,7 @@
 BLOCK = 32
 UNITS = 288
 MESH = pl.DeviceIdType.MESH
-LAG = 5
+LAG = 8
 NEAR = 4
 
 
@@ -71,18 +71,20 @@
     return jnp.where(blocks < 0.0, -level, level)
 
 
-def layer_kernel(passes, chunks, width, *refs):
+def layer_kernel(passes, turns, chunks, width, *refs):
     place_ref, lane_ref, raw_ref, up_ref, down_ref, out_ref = refs[:6]
     gather = refs[6:6 + passes]
     (x_ref, moved, blocks, panel, near, mine, hand, far, hid, total, own, parts, up_buf, down_buf,
      keep_sem, gather_send, gather_recv, moved_send, moved_recv, relay_send, relay_recv, up_sem, down_sem, near_send, near_recv,
      far_send, far_recv, hid_send, hid_recv, part_send, part_recv) = refs[6 + passes:]
-    items = passes * chunks
+    items = turns * chunks
+    split = turns // passes
     half = hand.shape[1]
     cols, seg = own.shape[1], own.shape[2]
     units, lanes = blocks.shape[2], blocks.shape[4]
     local = x_ref.shape[1]
     piece = lanes // passes
+    small = piece // split
     columns = out_ref.shape[1]
     row, col = lax.axis_index("row"), lax.axis_index("col")
     core = lax.rem(row, 2)
@@ -216,13 +218,15 @@
     def lay(p):
         for k in range(4):
             origin = (row, partner, across, sibling)[k]
-            at = (half if k >= 2 else 0) + lax.div(origin, 2) * piece
+            at = (half if k >= 2 else 0) + lax.div(origin, 2) * small
 
             def one(j, carry):
                 tile = blocks[p, k, pl.ds(4 * j, 4)].reshape(4 * BLOCK, lanes).T
                 for q in range(passes):
                     chunk = pl.ds(pl.multiple_of(q * units * BLOCK + 4 * BLOCK * j, 128), 4 * BLOCK)
-                    panel[p, pl.ds(pl.multiple_of(at, piece), piece), chunk] = tile[q * piece:(q + 1) * piece]
+                    for i in range(split):
+                        first = q * piece + i * small
+                        panel[p * split + i, pl.ds(pl.multiple_of(at, small), small), chunk] = tile[first:first + small]
                 return carry
 
             lax.fori_loop(0, units // 4, one, 0)
@@ -257,10 +261,10 @@
 
     def step(t, carry):
         for p in range(1, passes):
-            begin = (p - 1) * chunks + chunks // 2
-            pl.when(t == begin)(functools.partial(collect, p))
-            pl.when(t == begin + 3)(functools.partial(hand_on, p))
-            pl.when(t == p * chunks)(functools.partial(finish, p))
+            end = p * split * chunks
+            pl.when(t == end - (split * chunks) // 2)(functools.partial(collect, p))
+            pl.when(t == end - (split * chunks) // 3)(functools.partial(hand_on, p))
+            pl.when(t == end)(functools.partial(finish, p))
 
         @pl.when(t < items)
         def _():
@@ -318,9 +322,9 @@
                 p = lax.div(item, chunks)
                 for k in (*range(1, cols), 0):
                     target = lax.rem(col + k, cols)
-                    origin = lax.div(target, piece // seg)
-                    at = (lax.rem(origin + core, 2) * half + lax.div(origin, 2) * piece
-                          + lax.rem(target, piece // seg) * seg)
+                    origin = lax.div(target, small // seg)
+                    at = (lax.rem(origin + core, 2) * half + lax.div(origin, 2) * small
+                          + lax.rem(target, small // seg) * seg)
                     own[p, k] = total[pl.ds(pl.multiple_of(at, seg), seg), :].astype(jnp.bfloat16)
                     if k > 0:
                         to_part(p, k).start()
@@ -346,13 +350,13 @@
             for k in (1, 2):
                 for m in range(1, cols):
                     to_relay(p, k, m).wait_send()
-    for p in range(passes):
+    for p in range(turns):
         mixed = own[p, 0].astype(jnp.float32)
         for k in range(1, cols):
             to_part(p, k).wait_recv()
             mixed = mixed + parts[p, k].astype(jnp.float32)
         out_ref[p * seg:(p + 1) * seg, :] = mixed.astype(jnp.bfloat16)
-    for p in range(passes):
+    for p in range(turns):
         for k in range(1, cols):
             to_part(p, k).wait_send()
 
@@ -364,47 +368,48 @@
         local_units, lanes = values.shape[1] // BLOCK // passes, values.shape[0]
     depth, hidden = up_weight.shape
     columns = down_weight.shape[1]
-    tokens = 4 * lanes // passes
+    turns = 2 * passes if (lanes // passes) % 32 == 0 and passes > 1 else passes
+    tokens = 4 * lanes // turns
     units = depth // BLOCK // passes
     width = next(w for w in (512, 384, 256, 128) if hidden % w == 0)
     chunks = hidden // width
-    items = passes * chunks
+    items = turns * chunks
     half = tokens // 2
     seg = tokens // cols
-    flops = 2 * passes * tokens * hidden * (depth + columns)
+    flops = 2 * turns * tokens * hidden * (depth + columns)
     vmem = pl.BlockSpec(memory_space=pltpu.VMEM)
     smem = pl.BlockSpec(memory_space=pltpu.SMEM)
     hbm = pl.BlockSpec(memory_space=pl.ANY)
     dma = pltpu.SemaphoreType.DMA
     return pl.pallas_call(
-        functools.partial(layer_kernel, passes, chunks, width),
-        out_shape=jax.ShapeDtypeStruct((passes * seg, columns), jnp.bfloat16),
+        functools.partial(layer_kernel, passes, turns, chunks, width),
+        out_shape=jax.ShapeDtypeStruct((turns * seg, columns), jnp.bfloat16),
         in_specs=[smem, smem, vmem, hbm, hbm],
         out_specs=vmem,
         scratch_shapes=[pltpu.VMEM((cols * local_units, BLOCK, lanes), jnp.bfloat16)] * passes + [
             pltpu.VMEM((passes, local_units, BLOCK, lanes), jnp.bfloat16),
             pltpu.VMEM((passes, 3, units, BLOCK, lanes), jnp.bfloat16),
             pltpu.VMEM((passes, 4, units, BLOCK, lanes), jnp.bfloat16),
-            pltpu.VMEM((passes, tokens, depth), jnp.bfloat16),
+            pltpu.VMEM((turns, tokens, depth), jnp.bfloat16),
             pltpu.VMEM((NEAR, half, width), jnp.bfloat16),
             pltpu.VMEM((2, half, width), jnp.float32),
             pltpu.VMEM((items, half, width), jnp.bfloat16),
             pltpu.VMEM((items, half, width), jnp.bfloat16),
             pltpu.VMEM((items, 2, half, width), jnp.bfloat16),
             pltpu.VMEM((tokens, columns), jnp.float32),
-            pltpu.VMEM((passes, cols, seg, columns), jnp.bfloat16),
-            pltpu.VMEM((passes, cols, seg, columns), jnp.bfloat16),
+            pltpu.VMEM((turns, cols, seg, columns), jnp.bfloat16),
+            pltpu.VMEM((turns, cols, seg, columns), jnp.bfloat16),
             pltpu.VMEM((2, depth, width), jnp.bfloat16),
             pltpu.VMEM((2, width, columns), jnp.bfloat16),
             dma((passes,)), dma((passes, cols)), dma((passes, cols)), dma((passes, 3)), dma((passes, 3)),
             dma((passes, 2, cols)), dma((passes, 2, cols)),
             dma((2,)), dma((2,)), dma((NEAR,)), dma((items,)), dma((items,)), dma((items,)),
-            dma((items,)), dma((items,)), dma((passes, cols)), dma((passes, cols)),
+            dma((items,)), dma((items,)), dma((turns, cols)), dma((turns, cols)),
         ],
         compiler_params=pltpu.CompilerParams(
             collective_id=0, has_side_effects=True, vmem_limit_bytes=60 * 1024 * 1024),
         cost_estimate=pl.CostEstimate(flops=flops, transcendentals=0,
-                                      bytes_accessed=2 * passes * (up_weight.size + down_weight.size)),
+                                      bytes_accessed=2 * turns * (up_weight.size + down_weight.size)),
     )(place, lane, values, up_weight, down_weight)
 
 

time: 199 us -> 191 us (0.960)
  Pallas kernels: 192 us -> 185 us
    pallas_call x1, Pallas kernels: 192 us -> 185 us  [layer(): pl.pallas_call(functools.partial(layer_kernel, passes, turns, chunks, wid...]
where the time goes in v4:
time: 191 us; the launch traced here: 190 us
  Pallas kernels  185 us (97%)
  other arithmetic  2.84 us (1%)
  local copies, waits for them, and re-layouts  2.76 us (1%)
    pallas_call x1, Pallas kernels, layer(): pl.pallas_call(functools.partial(layer_kernel, passes, turns, chunks, wid...  185 us

profile of v4, /device:TPU:25, one launch (start us, length us, event | category | flops | bytes accessed | tf_op | source)
XLA Modules:
  0.0 190.4 jit_solution(11702072563704119367)
XLA Ops:
  0.0 0.7 copy.11
  0.7 0.1 reduce-window.17
  0.8 0.1 reduce.1
  0.9 0.7 sub.27
  1.6 0.8 select_reduce_fusion.3
  2.5 0.1 copy.10
  2.6 0.1 reduce-window.16
  2.7 0.1 reduce
  2.8 0.1 select_reduce_fusion.1
  2.9 0.2 select_reduce_fusion
  3.1 0.6 add_select_fusion
  3.7 184.8 %shard_map.55 = bf16[128,2304]{1,0:T(8,128)(2,1)} custom-call(s32[288]{0:T(512)} %get-tuple-element.8.refs_0_, s32[288]{0:T(512)} %get-tuple-element.7.refs_1_, bf16[128,2304]{1,0:T(8,128)(2,1)} %refs_2_.1, bf16[2304,9216]{1,0:T(8,128)(2,1)} %refs_3_.1, bf16[9216,2304]{1,0:T(8,128)(2,1)} %refs_4_.1), custom_call_target="tpu_custom_call" | custom-call | flops 43486543872 | bytes 339738624 | tf_op jit(solution)/shard_map/pallas_call | solution.py:384
  188.5 1.9 %copy.13 = bf16[128,2304]{1,0:T(8,128)(2,1)} copy(bf16[128,2304]{1,0:T(8,128)(2,1)} %shard_map.55) | data formatting | bytes 1179648
  (1 shorter events, 0.0 us)
